TPU v7x, 512 devices: a whole 4x4x16 slice. The times are simulated.
512 devices in a mesh: row: 32 (over x_hi, z), col: 16 (over x_lo, y, core).
Axes of the slice: x: 4 (x_hi: 2, x_lo: 2; x = x_hi * 2 + x_lo), y: 4, z: 16, core: 2. Of those that a mesh axis runs over, the one named last changes fastest.
Arguments:
- gradient: float32 [3584, 7168], P('row', 'col'), may hold values from -6 to 6
- moment: float32 [3584, 7168], P('row', 'col'), may hold values from -2 to 2
- second: float32 [3584, 7168], P('row', 'col'), may hold values from 0.05 to 2
- left_basis: bfloat16 [3584, 3584], P('row', 'col'), may hold values from -0.09375 to 0.09375
- right_basis: bfloat16 [7168, 7168], P('row', 'col'), may hold values from -0.0625 to 0.0625
Outputs:
- new_moment: float32 [3584, 7168], P('row', 'col')
- new_second: float32 [3584, 7168], P('row', 'col')
- update: float32 [3584, 7168], P('row', 'col')
All inputs are finite; a program needn't handle non-finite values.
Results may differ from a plain program's by a relative error of at most 0.022.
Values may be sent and summed in bfloat16 or wider, within the bound.
A program may use at most 64 MiB of HBM per device.

v0:
```python
import jax
import jax.numpy as jnp
from jax import lax
from jax.sharding import PartitionSpec as P

STEP = 100


beta_first = 0.9
beta_second = 0.99
epsilon_add = 1e-08


def multiply(matrix, column_block, summed_axis):
    return lax.dot_general(
        matrix, column_block, (((summed_axis,), (0,)), ((), ())), preferred_element_type=jnp.float32
    )


def contract_panel(local_rows, matrix, summed_axis):
    gathered = lax.all_gather(local_rows, "row", axis=0, tiled=True)
    return multiply(matrix, gathered, summed_axis)


def per_device(gradient, moment, second, left_basis, right_basis):
    low_gradient = gradient.astype(jnp.bfloat16)
    gradient_rows, left_rows = (
        lax.all_gather(low_gradient, "col", axis=1, tiled=True),
        lax.all_gather(left_basis, "col", axis=1, tiled=True),
    )
    basis_panel = lax.all_gather(right_basis, "row", axis=0, tiled=True)
    half_rotated = jnp.dot(gradient_rows, basis_panel, preferred_element_type=jnp.float32).astype(
        jnp.bfloat16
    )
    left_columns = lax.all_to_all(left_rows, "row", split_axis=1, concat_axis=0, tiled=True)
    rotated = contract_panel(half_rotated, left_columns, 0)
    new_moment = beta_first * moment + (1.0 - beta_first) * rotated
    new_second = beta_second * second + (1.0 - beta_second) * rotated * rotated
    first_fix = 1.0 - beta_first**STEP
    second_fix = 1.0 - beta_second**STEP
    direction = (new_moment / first_fix / (jnp.sqrt(new_second / second_fix) + epsilon_add)).astype(
        jnp.bfloat16
    )
    back_rotated = contract_panel(direction, left_rows, 1).astype(jnp.bfloat16)
    partial_value = lax.dot_general(
        back_rotated, basis_panel, (((1,), (1,)), ((), ())), preferred_element_type=jnp.float32
    )
    update = lax.psum_scatter(
        partial_value.astype(jnp.bfloat16), "col", scatter_dimension=1, tiled=True
    ).astype(jnp.float32)
    return (new_moment, new_second, update)


def solution(mesh):
    return jax.shard_map(
        per_device,
        mesh=mesh,
        in_specs=(
            P("row", "col"),
            P("row", "col"),
            P("row", "col"),
            P("row", "col"),
            P("row", "col"),
        ),
        out_specs=(P("row", "col"), P("row", "col"), P("row", "col")),
        check_vma=False,
    )
```

profile of v0, /device:TPU:4, one launch (start us, length us, event | category | flops | bytes accessed | tf_op | source)
XLA Modules:
  0.0 666.9 jit_solution(14530850597973135193)
XLA Ops:
  7.2 1.7 copy.18
  9.0 0.7 all-gather.7.cloned.1.call-update
  9.8 46.4 %all-gather.5.cloned.1.call-done = bf16[112,7168]{0,1:T(8,128)(2,1)} async-done(((bf16[112,448]{0,1:T(8,128)(2,1)}), bf16[112,7168]{0,1:T(8,128)(2,1)}) %all-gather.5.cloned.1.call-update) | async-done | bytes 1605648 | tf_op jit(solution)/shard_map/all_gather | solution.py:28
  56.1 187.1 %all-gather.7.cloned.1.call-done = bf16[7168,448]{1,0:T(8,128)(2,1)} async-done(((bf16[224,448]{1,0:T(8,128)(2,1)}), bf16[7168,448]{1,0:T(8,128)(2,1)}) %all-gather.7.cloned.1.call-update) | async-done | bytes 6422544 | tf_op jit(solution)/shard_map/all_gather | solution.py:31
  243.2 5.6 convolution_convert_fusion.2
  248.8 0.1 copy.19
  248.9 24.4 %all_gather.18 = bf16[112,3584]{0,1:T(8,128)(2,1)} all-gather(bf16[112,224]{0,1:T(8,128)(2,1)S(1)} %copy.19), channel_id=1, replica_groups=mesh['row'=32,'col'=16] {'col'}, dimensions={1}, use_global_device_ids=true | all-gather | bytes 852992 | tf_op jit(solution)/shard_map/all_gather | solution.py:29
  273.3 11.2 %all-to-all-start = ((bf16[112,32,112]{0,2,1:T(8,128)(2,1)}), bf16[112,32,112]{0,2,1:T(8,128)(2,1)S(1)}, u32[]{:S(2)}, u32[]{:S(2)}) async-start(bf16[112,32,112]{0,2,1:T(8,128)(2,1)} %bitcast), calls=%async_computation | async-start | bytes 1835008 | tf_op jit(solution)/shard_map/all_to_all | solution.py:35
  284.6 0.1 copy.17
  284.7 0.1 copy.21
  284.9 49.9 %all-to-all-done = bf16[112,32,112]{0,2,1:T(8,128)(2,1)S(1)} async-done(((bf16[112,32,112]{0,2,1:T(8,128)(2,1)}), bf16[112,32,112]{0,2,1:T(8,128)(2,1)S(1)}, u32[]{:S(2)}, u32[]{:S(2)}) %all-to-all-start) | async-done | bytes 802848 | tf_op jit(solution)/shard_map/all_to_all | solution.py:35
  334.8 0.2 copy.20
  335.0 1.9 all_to_all.17
  336.9 82.7 %all-gather.9.cloned.1.call-done = bf16[3584,448]{1,0:T(8,128)(2,1)} async-done(((bf16[112,448]{1,0:T(8,128)(2,1)}), bf16[3584,448]{1,0:T(8,128)(2,1)}) %all-gather.9.cloned.1.call-update) | async-done | bytes 3211280 | tf_op jit(solution)/shard_map/all_gather | solution.py:21
  419.6 3.2 divide_convert_fusion
  422.8 0.8 copy.22
  423.7 155.6 %all-gather.11.cloned.1.call-done = bf16[3584,448]{1,0:T(8,128)(2,1)} async-done(((bf16[112,448]{1,0:T(8,128)(2,1)}), bf16[3584,448]{1,0:T(8,128)(2,1)}) %all-gather.11.cloned.1.call-update) | async-done | bytes 3211280 | tf_op jit(solution)/shard_map/all_gather | solution.py:21
  579.3 9.4 %convolution_convert_fusion = bf16[112,7168]{1,0:T(8,128)(2,1)S(1)} fusion(bf16[7168,448]{1,0:T(8,128)(2,1)} %all-gather.7.cloned.1.call-done, bf16[3584,448]{1,0:T(8,128)(2,1)} %all-gather.11.cloned.1.call-done, bf16[112,3584]{0,1:T(8,128)(2,1)} %all_gather.18), kind=kOutput, calls=%fused_computation | convolution fusion | flops 1079837696 | bytes 12042240 | tf_op jit(solution)/shard_map/dot_general | solution.py:45
  588.6 2.3 copy.25
  591.0 0.8 copy.23
  591.8 0.8 copy.24
  592.6 66.0 %reduce-scatter.4.cloned.1.call-done = bf16[448,112]{1,0:T(8,128)(2,1)} async-done(((bf16[7168,112]{1,0:T(8,128)(2,1)}), bf16[448,112]{1,0:T(8,128)(2,1)}) %reduce-scatter.4.cloned.1.call-update) | async-done | bytes 100368
  658.6 1.0 copy.26
  659.6 0.7 convert_element_type.24
  (15 shorter events, 0.3 us)
Async XLA Ops:
  7.2 49.0 %all-gather.5.cloned.1.call-start = ((), (), s32[]{:S(2)}) async-start(), calls=%async_computation.2 | async-start | bytes 1949696 | tf_op jit(solution)/shard_map/all_gather | solution.py:28
  8.9 234.2 %all-gather.7.cloned.1.call-start = ((), (), s32[]{:S(2)}) async-start(), calls=%async_computation.3 | async-start | bytes 7569408 | tf_op jit(solution)/shard_map/all_gather | solution.py:31
  9.7 239.1 %copy-start.2 = (bf16[112,224]{1,0:T(8,128)(2,1)S(1)}, bf16[112,224]{1,0:T(8,128)(2,1)}, u32[]{:S(2)}) copy-start(bf16[112,224]{1,0:T(8,128)(2,1)} %param.8) | copy-start | bytes 150532
  9.7 274.9 %copy-start = (f32[112,448]{1,0:T(8,128)S(1)}, f32[112,448]{1,0:T(8,128)}, u32[]{:S(2)}) copy-start(f32[112,448]{1,0:T(8,128)} %param.6) | copy-start | bytes 602116
  9.7 275.0 %copy-start.1 = (f32[112,448]{1,0:T(8,128)S(1)}, f32[112,448]{1,0:T(8,128)}, u32[]{:S(2)}) copy-start(f32[112,448]{1,0:T(8,128)} %param.7) | copy-start | bytes 602116
  9.7 409.9 %all-gather.9.cloned.1.call-start = ((), (), s32[]{:S(2)}) async-start(), calls=%async_computation.4 | async-start | bytes 3784704 | tf_op jit(solution)/shard_map/all_gather | solution.py:21
  273.3 61.5 %all-to-all-start = ((bf16[112,32,112]{0,2,1:T(8,128)(2,1)}), bf16[112,32,112]{0,2,1:T(8,128)(2,1)S(1)}, u32[]{:S(2)}, u32[]{:S(2)}) async-start(bf16[112,32,112]{0,2,1:T(8,128)(2,1)} %bitcast), calls=%async_computation | async-start | bytes 1835008 | tf_op jit(solution)/shard_map/all_to_all | solution.py:35
  284.5 294.7 %all-gather.11.cloned.1.call-start = ((), (), s32[]{:S(2)}) async-start(), calls=%async_computation.5 | async-start | bytes 3784704 | tf_op jit(solution)/shard_map/all_gather | solution.py:21
  423.6 235.0 %reduce-scatter.4.cloned.1.call-start = ((), (), s32[]{:S(2)}) async-start(), calls=%async_computation.6 | async-start | bytes 1949696
Sparse Core Ops, SparseCore 0:
  10.7 45.3 all-gather.4
  59.2 183.9 all-gather.6
  248.9 170.6 all-gather.8
  423.7 155.4 all-gather.10
  591.1 67.5 reduce-scatter.3
where the time goes:
time: 667 us
  waiting for transfers between devices  588 us (88%)
  blocking collectives  24.4 us (4%)
  matrix products  18.2 us (3%)
  between operations  13.9 us (2%)
  starting transfers between devices  11.4 us (2%)
  local copies, waits for them, and re-layouts  9.87 us (1%)
    all_gather x2, waiting for transfers between devices, contract_panel(): gathered = lax.all_gather(local_rows, 'row', axis=0, tiled=True)  238 us
    all_gather x1, waiting for transfers between devices, per_device(): basis_panel = lax.all_gather(right_basis, 'row', axis=0, tiled=True)  187 us
    unnamed x6, waiting for transfers between devices  66.8 us
    all_to_all x1, waiting for transfers between devices, per_device(): lax.all_to_all(left_rows, 'row', split_axis=1, concat_axis=0, tiled=True)  49.9 us
    all_gather x1, waiting for transfers between devices, per_device(): lax.all_gather(low_gradient, 'col', axis=1, tiled=True)  46.4 us
    all_gather x1, blocking collectives, per_device(): lax.all_gather(left_basis, 'col', axis=1, tiled=True)  24.4 us
  transfers between devices with their start and end apart: 6, of which 6 were waited for; matrix products, arithmetic and copies ran while one was open for 0% of the time, Pallas kernels for 0%

commit v1 on v0

v1 whole, which is shorter than its diff:
```python
import functools

import jax
import jax.numpy as jnp
from jax import lax
from jax.experimental import pallas as pl
from jax.experimental.pallas import tpu as pltpu
from jax.sharding import PartitionSpec as P

STEP = 100


beta_first = 0.9
beta_second = 0.99
epsilon_add = 1e-08

F32 = jnp.float32
BF16 = jnp.bfloat16


def optimizer_kernel(
    Z, Y,
    g_ref, m_ref, v_ref, l_ref, r_ref,
    nm_ref, nv_ref, up_ref,
    g_own, g_all, l_all, r_all, part, from_a, from_b, t_own, t_all,
    x_out, x_in, d_all, b_out, b_in, sib_out, sib_in, u_out, u_in,
    g_sem, ls_sem, lr_sem, lfs_sem, lfr_sem, rs_sem, rr_sem,
    tas_sem, tar_sem, tbs_sem, tbr_sem, ts_sem, tr_sem, tfs_sem, tfr_sem,
    x_sem, d_sem_s, d_sem_r, b_sem, ss_sem, sr_sem, us_sem, ur_sem,
):
    C = 2
    K = Y * C
    A, B = Z // 2, Z - 1 - Z // 2
    mr = g_ref.shape[0]
    row, col = lax.axis_index("row"), lax.axis_index("col")
    xh, z = row // Z, lax.rem(row, Z)
    core = lax.rem(col, C)
    y = lax.rem(col // C, Y)
    xl = col // (C * Y)
    sg = 1 - 2 * core
    mine = xh == xl

    def wrap(value):
        return lax.rem(value + 4 * Z, Z)

    def device(dxh, dz, dxl, dy, dcore):
        return {"row": dxh * Z + dz, "col": (dxl * Y + dy) * C + dcore}

    ahead = device(xh, wrap(z + sg), xl, y, core)
    behind = device(xh, wrap(z - sg), xl, y, core)
    partner = device(1 - xh, z, xl, y, core)
    sibling = device(xh, z, xl, y, 1 - core)

    def copy(src, dst, send, recv, target):
        return pltpu.make_async_remote_copy(
            src_ref=src, dst_ref=dst, send_sem=send, recv_sem=recv,
            device_id=target, device_id_type=pl.DeviceIdType.MESH,
        )

    barrier = pltpu.get_barrier_semaphore()

    def greet(target):
        pl.semaphore_signal(barrier, inc=1, device_id=target, device_id_type=pl.DeviceIdType.MESH)

    greet(ahead)
    greet(behind)
    for other in range(1, 4 * K):
        place = lax.rem(xh * 2 * K + col + other, 4 * K)
        greet({"row": (place // (2 * K)) * Z + z, "col": lax.rem(place, 2 * K)})

    g_own[...] = g_ref[...].astype(BF16)
    rows_me = pl.ds(pl.multiple_of(xh * mr, mr), mr)
    g_all[rows_me, :] = g_own[...]
    r_all[z] = r_ref[...]
    slot_me = y * C + core

    @pl.when(mine)
    def _():
        l_all[slot_me, rows_me, :] = l_ref[...]

    pl.semaphore_wait(barrier, 4 * K + 1)

    def to_chips(t):
        dxl, dy = t // Y, t % Y
        here = jnp.logical_and(mine, jnp.logical_and(dxl == xl, dy == y))
        return device(xl, z, dxl, dy, core), jnp.logical_not(here)

    def from_chips(t):
        sxh, sy = t // Y, t % Y
        here = jnp.logical_and(mine, jnp.logical_and(sxh == xh, sy == y))
        return sxh, sy, jnp.logical_not(here)

    def spread(src, dst, send, recv):
        for t in range(2 * Y):
            target, remote = to_chips(t)

            @pl.when(remote)
            def _():
                copy(src, dst.at[slot_me, rows_me, :], send.at[t], recv.at[xh * Y + y], target).start()

    def spread_wait(src, dst, send, recv):
        for t in range(2 * Y):
            target, remote = to_chips(t)

            @pl.when(remote)
            def _():
                copy(src, dst.at[slot_me, rows_me, :], send.at[t], recv.at[0], target).wait_send()

    def share_copy(dst, t, send, recv, c):
        sxh, sy = t // Y, t % Y
        place = dst.at[sy * C + c, pl.ds(sxh * mr, mr), :]
        return copy(place, place, send.at[t], recv.at[t], sibling)

    def share(src, dst, send, recv, fsend, frecv):
        for t in range(2 * Y):
            sxh, sy, remote = from_chips(t)
            place = dst.at[sy * C + core, pl.ds(sxh * mr, mr), :]

            @pl.when(remote)
            def _():
                copy(place, place, send.at[0], recv.at[t], sibling).wait_recv()

            share_copy(dst, t, fsend, frecv, core).start()

    def share_wait(dst, fsend, frecv):
        for t in range(2 * Y):
            share_copy(dst, t, fsend, frecv, 1 - core).wait_recv()

    def share_sent(dst, fsend, frecv):
        for t in range(2 * Y):
            share_copy(dst, t, fsend, frecv, core).wait_send()

    def r_piece(owner, chunk):
        return r_all.at[owner, pl.ds(chunk * mr, mr), :]

    chunks = r_ref.shape[0] // mr

    def r_copy(side, s, chunk):
        if side == 0:
            piece, target = r_piece(wrap(z - sg * (s - 1)), chunk), ahead
        else:
            piece, target = r_piece(wrap(z + sg * (s - 1)), chunk), behind
        index = ((side * A) + s - 1) * chunks + chunk
        return copy(piece, piece, rs_sem.at[index], rr_sem.at[index], target)

    def r_arrival(side, s, chunk):
        piece = r_piece(wrap(z - sg * s) if side == 0 else wrap(z + sg * s), chunk)
        index = ((side * A) + s - 1) * chunks + chunk
        copy(piece, piece, rs_sem.at[index], rr_sem.at[index], ahead).wait_recv()

    def r_step(n):
        s, chunk = n // chunks + 1, n % chunks
        for side, last in ((0, A), (1, B)):
            if s <= last:
                r_arrival(side, s, chunk)
                if s < last:
                    r_copy(side, s + 1, chunk).start()

    for chunk in range(chunks):
        if A:
            r_copy(0, 1, chunk).start()
        if B:
            r_copy(1, 1, chunk).start()
        if chunk == 0:
            g_copy = copy(g_own, g_all.at[rows_me, :], g_sem.at[0], g_sem.at[1], partner)
            g_copy.start()
            spread(l_ref, l_all, ls_sem, lr_sem)
    share(l_ref, l_all, ls_sem, lr_sem, lfs_sem, lfr_sem)
    r_step(0)
    g_copy.wait_recv()
    share_wait(l_all, lfs_sem, lfr_sem)

    per = Z // K

    def part_body(i, _):
        k = lax.rem(z // per + K // 2 + i, K)
        value = lax.dot_general(
            l_all[k], g_all[...], (((0,), (0,)), ((), ())), preferred_element_type=F32
        ).astype(BF16)
        for j in range(per):
            part[k * per + j] = value[j * mr:(j + 1) * mr, :]
        return 0

    lax.fori_loop(0, K, part_body, 0)

    def t_copy(side, s):
        if side == 0:
            d = wrap(z + sg * (A + 1 - s))
            return d, copy(part.at[d], from_a.at[s - 1], tas_sem.at[s - 1], tar_sem.at[s - 1], ahead)
        d = wrap(z - sg * (B + 1 - s))
        return d, copy(part.at[d], from_b.at[s - 1], tbs_sem.at[s - 1], tbr_sem.at[s - 1], behind)

    steps = A * chunks
    done = 1
    for s in range(1, A + 1):
        for side, last, came in ((0, A, from_a), (1, B, from_b)):
            if s <= last:
                d, send = t_copy(side, s)
                if s > 1:
                    t_copy(side, s - 1)[1].wait_recv()
                    part[d] = (part[d].astype(F32) + came[s - 2].astype(F32)).astype(BF16)
                send.start()
        if done < steps:
            r_step(done)
            done += 1
    total = part[z].astype(F32)
    if B:
        t_copy(1, B)[1].wait_recv()
        total = total + from_b[B - 1].astype(F32)
    t_copy(0, A)[1].wait_recv()
    total = total + from_a[A - 1].astype(F32)
    t_own[...] = total.astype(BF16)

    @pl.when(mine)
    def _():
        t_all[slot_me, rows_me, :] = t_own[...]

    spread(t_own, t_all, ts_sem, tr_sem)
    half = (steps - done) // 2
    while done < steps - half:
        r_step(done)
        done += 1
    share(t_own, t_all, ts_sem, tr_sem, tfs_sem, tfr_sem)
    while done < steps:
        r_step(done)
        done += 1
    share_wait(t_all, tfs_sem, tfr_sem)

    nc = r_ref.shape[1]

    def r_block(k):
        return r_all[pl.ds(k * per, per)].reshape(per * r_ref.shape[0], nc)

    acc = jnp.zeros((2 * mr, nc), F32)
    for k in range(K):
        acc = acc + jnp.dot(t_all[k], r_block(k), preferred_element_type=F32)
    x_out[...] = acc
    rows_other = pl.ds(pl.multiple_of((1 - xh) * mr, mr), mr)
    b_out[0:mr, :] = x_out[rows_other, :].astype(BF16)
    x_copy = copy(b_out.at[0:mr, :], x_in, x_sem.at[0], x_sem.at[1], partner)
    x_copy.start()
    x_copy.wait()
    rotated = x_out[rows_me, :] + x_in[...].astype(F32)
    new_moment = beta_first * m_ref[...] + (1.0 - beta_first) * rotated
    new_second = beta_second * v_ref[...] + (1.0 - beta_second) * rotated * rotated
    nm_ref[...] = new_moment
    nv_ref[...] = new_second
    first_fix = 1.0 - beta_first**STEP
    second_fix = 1.0 - beta_second**STEP
    direction = new_moment / first_fix / (jnp.sqrt(new_second / second_fix) + epsilon_add)

    def d_piece(owner):
        return d_all.at[owner // per, pl.ds(pl.multiple_of(lax.rem(owner, per) * mr, mr), mr), :]

    d_all[z // per, pl.ds(pl.multiple_of(lax.rem(z, per) * mr, mr), mr), :] = direction.astype(BF16)

    def d_copy(side, s):
        owner, target = (wrap(z - sg * (s - 1)), ahead) if side == 0 else (wrap(z + sg * (s - 1)), behind)
        index = side * A + s - 1
        piece = d_piece(owner)
        return copy(piece, piece, d_sem_s.at[index], d_sem_r.at[index], target)

    def d_arrival(side, s):
        piece = d_piece(wrap(z - sg * s) if side == 0 else wrap(z + sg * s))
        index = side * A + s - 1
        copy(piece, piece, d_sem_s.at[index], d_sem_r.at[index], ahead).wait_recv()

    for side, last in ((0, A), (1, B)):
        if last:
            d_copy(side, 1).start()
    for s in range(1, A + 1):
        for side, last in ((0, A), (1, B)):
            if s <= last:
                d_arrival(side, s)
                if s < last:
                    d_copy(side, s + 1).start()

    acc = jnp.zeros((2 * mr, nc), F32)
    for k in range(K):
        acc = acc + jnp.dot(l_all[k], d_all[k], preferred_element_type=F32)
    b_out[...] = acc.astype(BF16)
    b_copy = copy(b_out, b_in, b_sem.at[0], b_sem.at[1], partner)
    b_copy.start()
    b_copy.wait_recv()
    back = (acc + b_in[...].astype(F32)).astype(BF16)
    x_out[...] = back.astype(F32)

    def update_block(k):
        return lax.dot_general(
            x_out[...].astype(BF16), r_block(k), (((1,), (1,)), ((), ())), preferred_element_type=F32
        )

    def sib_copy(j):
        return copy(sib_out.at[j], sib_in.at[j], ss_sem.at[j], sr_sem.at[j], sibling)

    for j in range(Y):
        sib_out[j] = update_block(j * C + 1 - core).astype(BF16)
        sib_copy(j).start()

    def u_copy(t):
        txh, ty = t // Y, t % Y
        here = jnp.logical_and(mine, jnp.logical_and(txh == xh, ty == y))
        made = copy(
            u_out.at[ty, pl.ds(txh * mr, mr), :], u_in.at[xl * Y + y],
            us_sem.at[t], ur_sem.at[xl * Y + y], device(txh, z, xh, ty, core),
        )
        return made, here

    for j in range(Y):
        value = update_block(j * C + core)
        sib_copy(j).wait_recv()
        u_out[j] = (value + sib_in[j].astype(F32)).astype(BF16)
        for txh in range(2):
            made, here = u_copy(txh * Y + j)

            @pl.when(jnp.logical_not(here))
            def _():
                made.start()

    @pl.when(mine)
    def _():
        u_in[xl * Y + y] = u_out[y, rows_me, :]

    total = jnp.zeros((mr, nc), F32)
    for t in range(2 * Y):
        here = jnp.logical_and(mine, jnp.logical_and(t // Y == xl, t % Y == y))

        @pl.when(jnp.logical_not(here))
        def _():
            copy(u_in.at[t], u_in.at[t], us_sem.at[0], ur_sem.at[t], sibling).wait_recv()

        total = total + u_in[t].astype(F32)
    up_ref[...] = total

    g_copy.wait_send()
    b_copy.wait_send()
    spread_wait(l_ref, l_all, ls_sem, lr_sem)
    spread_wait(t_own, t_all, ts_sem, tr_sem)
    share_sent(l_all, lfs_sem, lfr_sem)
    share_sent(t_all, tfs_sem, tfr_sem)
    for side, last in ((0, A), (1, B)):
        for s in range(1, last + 1):
            for chunk in range(chunks):
                r_copy(side, s, chunk).wait_send()
            t_copy(side, s)[1].wait_send()
            d_copy(side, s).wait_send()
    for j in range(Y):
        sib_copy(j).wait_send()
    for t in range(2 * Y):
        made, here = u_copy(t)

        @pl.when(jnp.logical_not(here))
        def _():
            made.wait_send()


def per_device(Z, Y, gradient, moment, second, left_basis, right_basis):
    mr, nc = gradient.shape
    K = 2 * Y
    A, B = Z // 2, Z - 1 - Z // 2
    rr = right_basis.shape[0]
    lc = left_basis.shape[1]
    per = Z // K
    chunks = rr // mr
    V = pltpu.VMEM
    DMA = pltpu.SemaphoreType.DMA
    vmem = pl.BlockSpec(memory_space=pltpu.VMEM)
    out = jax.ShapeDtypeStruct((mr, nc), F32)
    return pl.pallas_call(
        functools.partial(optimizer_kernel, Z, Y),
        out_shape=(out, out, out),
        in_specs=[vmem] * 5,
        out_specs=(vmem, vmem, vmem),
        scratch_shapes=[
            V((mr, nc), BF16),
            V((2 * mr, nc), BF16),
            V((K, 2 * mr, lc), BF16),
            V((Z, rr, nc), BF16),
            V((Z, mr, nc), BF16),
            V((A, mr, nc), BF16),
            V((max(B, 1), mr, nc), BF16),
            V((mr, nc), BF16),
            V((K, 2 * mr, nc), BF16),
            V((2 * mr, nc), F32),
            V((mr, nc), BF16),
            V((K, per * mr, nc), BF16),
            V((2 * mr, nc), BF16),
            V((2 * mr, nc), BF16),
            V((Y, 2 * mr, nc), BF16),
            V((Y, 2 * mr, nc), BF16),
            V((Y, 2 * mr, nc), BF16),
            V((2 * Y, mr, nc), BF16),
            DMA((2,)),
            DMA((2 * Y,)), DMA((2 * Y,)), DMA((2 * Y,)), DMA((2 * Y,)),
            DMA(((A + B) * chunks,)), DMA(((A + B) * chunks,)),
            DMA((A,)), DMA((A,)), DMA((max(B, 1),)), DMA((max(B, 1),)),
            DMA((2 * Y,)), DMA((2 * Y,)), DMA((2 * Y,)), DMA((2 * Y,)),
            DMA((2,)),
            DMA((A + B,)), DMA((A + B,)),
            DMA((2,)),
            DMA((Y,)), DMA((Y,)),
            DMA((2 * Y,)), DMA((2 * Y,)),
        ],
        compiler_params=pltpu.CompilerParams(
            collective_id=0, has_side_effects=True, vmem_limit_bytes=48 * 1024 * 1024
        ),
    )(gradient, moment, second, left_basis, right_basis)


def solution(mesh):
    Z, Y = mesh.shape["row"] // 2, mesh.shape["col"] // 4
    return jax.shard_map(
        functools.partial(per_device, Z, Y),
        mesh=mesh,
        in_specs=(
            P("row", "col"),
            P("row", "col"),
            P("row", "col"),
            P("row", "col"),
            P("row", "col"),
        ),
        out_specs=(P("row", "col"), P("row", "col"), P("row", "col")),
        check_vma=False,
    )
```

time: 667 us -> 169 us (0.25)
  the two profiles are of different devices: /device:TPU:4 before, /device:TPU:29 now
where the time goes in v1:
time: 169 us; the launch traced here: 168 us
  Pallas kernels  161 us (95%)
  local copies, waits for them, and re-layouts  6.63 us (4%)
    pallas_call x1, Pallas kernels, per_device(): pl.pallas_call(functools.partial(optimizer_kernel, Z, Y), out_shape=(out,...  161 us
    unnamed x13, local copies, waits for them, and re-layouts  6.63 us

profile of v1, /device:TPU:29, one launch (start us, length us, event | category | flops | bytes accessed | tf_op | source)
XLA Modules:
  0.0 168.3 jit_solution(7678822340935539821)
XLA Ops:
  0.6 0.0 copy-start
  0.6 0.9 copy-done
  1.6 0.0 copy-start.1
  1.6 0.9 copy-done.1
  2.5 0.0 copy-start.2
  2.5 0.9 copy-done.2
  3.4 0.0 copy-start.3
  3.5 0.9 copy-done.3
  4.4 0.0 copy-start.4
  4.4 0.8 copy-done.4
  5.2 161.0 %shard_map.76 = (f32[112,448]{1,0:T(8,128)S(1)}, f32[112,448]{1,0:T(8,128)S(1)}, f32[112,448]{1,0:T(8,128)S(1)}) custom-call(f32[112,448]{1,0:T(8,128)S(1)} %copy-done, f32[112,448]{1,0:T(8,128)S(1)} %copy-done.1, f32[112,448]{1,0:T(8,128)S(1)} %copy-done.2, bf16[112,224]{1,0:T(8,128)(2,1)S(1)} %copy-done.4, bf16[224,448]{1,0:T(8,128)(2,1)S(1)} %copy-done.3), custom_call_target="tpu_custom_call" | custom-call | tf_op jit(solution)/shard_map/pallas_call | solution.py:369
  166.2 0.7 copy.11
  166.9 0.7 copy.12
  167.6 0.7 copy.13
Async XLA Ops:
  0.6 0.9 copy-start
  1.6 0.9 copy-start.1
  2.5 0.9 copy-start.2
  3.4 0.9 copy-start.3
  4.4 0.8 copy-start.4

commit v2 on v1

v2 whole, which is shorter than its diff:
```python
import functools

import jax
import jax.numpy as jnp
from jax import lax
from jax.experimental import pallas as pl
from jax.experimental.pallas import tpu as pltpu
from jax.sharding import PartitionSpec as P

STEP = 100
R_START = 1
E_EARLY = 0
R_FIRST = True
R_FILL = (1,)


beta_first = 0.9
beta_second = 0.99
epsilon_add = 1e-08

F32 = jnp.float32
BF16 = jnp.bfloat16


def optimizer_kernel(
    Z, Y,
    g_ref, m_ref, v_ref, l_ref, r_ref,
    nm_ref, nv_ref, up_ref,
    g_own, g_all, l_all, r_all, part, from_a, from_b, t_own, t_all,
    g_in, m_in, v_in, l_in, x_out, f_out, f_in, d_own, d_all, b_out, b_in, sib_out, sib_in, u_out, u_in,
    in_sem, out_sem, g_sem, ls_sem, lr_sem, lfs_sem, lfr_sem, rs_sem, rr_sem,
    tas_sem, tar_sem, tbs_sem, tbr_sem, ts_sem, tr_sem, tfs_sem, tfr_sem,
    x_sem, d_sem_s, d_sem_r, b_sem, ss_sem, sr_sem, us_sem, ur_sem, mv_sem,
):
    C = 2
    K = Y * C
    A, B = Z // 2, Z - 1 - Z // 2
    mr = g_ref.shape[0]
    row, col = lax.axis_index("row"), lax.axis_index("col")
    xh, z = row // Z, lax.rem(row, Z)
    core = lax.rem(col, C)
    y = lax.rem(col // C, Y)
    xl = col // (C * Y)
    sg = 1 - 2 * core
    rows_me = pl.ds(pl.multiple_of(xh * mr, mr), mr)
    mine = xh == xl

    def wrap(value):
        return lax.rem(value + 4 * Z, Z)

    def device(dxh, dz, dxl, dy, dcore):
        return {"row": dxh * Z + dz, "col": (dxl * Y + dy) * C + dcore}

    ahead = device(xh, wrap(z + sg), xl, y, core)
    behind = device(xh, wrap(z - sg), xl, y, core)
    partner = device(1 - xh, z, xl, y, core)
    sibling = device(xh, z, xl, y, 1 - core)

    def copy(src, dst, send, recv, target):
        return pltpu.make_async_remote_copy(
            src_ref=src, dst_ref=dst, send_sem=send, recv_sem=recv,
            device_id=target, device_id_type=pl.DeviceIdType.MESH,
        )

    barrier = pltpu.get_barrier_semaphore()

    def greet(target):
        pl.semaphore_signal(barrier, inc=1, device_id=target, device_id_type=pl.DeviceIdType.MESH)

    loads = [
        pltpu.make_async_copy(src, dst, in_sem.at[i])
        for i, (src, dst) in enumerate(
            ((g_ref, g_in), (l_ref, l_in), (r_ref, r_all.at[z]), (m_ref, m_in.at[rows_me, :]), (v_ref, v_in.at[rows_me, :]))
        )
    ]
    for load in loads:
        load.start()
    greet(ahead)
    greet(behind)
    for other in range(1, 4 * K):
        place = lax.rem(xh * 2 * K + col + other, 4 * K)
        greet({"row": (place // (2 * K)) * Z + z, "col": lax.rem(place, 2 * K)})

    loads[0].wait()
    g_own[...] = g_in[...].astype(BF16)
    g_all[rows_me, :] = g_own[...]
    slot_me = y * C + core

    loads[1].wait()

    @pl.when(mine)
    def _():
        l_all[slot_me, rows_me, :] = l_in[...]

    pl.semaphore_wait(barrier, 4 * K + 1)

    def to_chips(t):
        dxl, dy = t // Y, t % Y
        here = jnp.logical_and(mine, jnp.logical_and(dxl == xl, dy == y))
        return device(xl, z, dxl, dy, core), jnp.logical_not(here)

    def from_chips(t):
        sxh, sy = t // Y, t % Y
        here = jnp.logical_and(mine, jnp.logical_and(sxh == xh, sy == y))
        return sxh, sy, jnp.logical_not(here)

    def spread(src, dst, send, recv):
        for t in range(2 * Y):
            target, remote = to_chips(t)

            @pl.when(remote)
            def _():
                copy(src, dst.at[slot_me, rows_me, :], send.at[t], recv.at[xh * Y + y], target).start()

    def spread_wait(src, dst, send, recv):
        for t in range(2 * Y):
            target, remote = to_chips(t)

            @pl.when(remote)
            def _():
                copy(src, dst.at[slot_me, rows_me, :], send.at[t], recv.at[0], target).wait_send()

    def share_copy(dst, t, send, recv, c):
        sxh, sy = t // Y, t % Y
        place = dst.at[sy * C + c, pl.ds(sxh * mr, mr), :]
        return copy(place, place, send.at[t], recv.at[t], sibling)

    def share(src, dst, send, recv, fsend, frecv):
        for t in range(2 * Y):
            sxh, sy, remote = from_chips(t)
            place = dst.at[sy * C + core, pl.ds(sxh * mr, mr), :]

            @pl.when(remote)
            def _():
                copy(place, place, send.at[0], recv.at[t], sibling).wait_recv()

            share_copy(dst, t, fsend, frecv, core).start()

    def share_wait(dst, fsend, frecv):
        for t in range(2 * Y):
            share_copy(dst, t, fsend, frecv, 1 - core).wait_recv()

    def share_sent(dst, fsend, frecv):
        for t in range(2 * Y):
            share_copy(dst, t, fsend, frecv, core).wait_send()

    def r_piece(owner, chunk):
        return r_all.at[owner, pl.ds(chunk * mr, mr), :]

    chunks = r_ref.shape[0] // mr

    def r_copy(side, s, chunk):
        if side == 0:
            piece, target = r_piece(wrap(z - sg * (s - 1)), chunk), ahead
        else:
            piece, target = r_piece(wrap(z + sg * (s - 1)), chunk), behind
        index = ((side * A) + s - 1) * chunks + chunk
        return copy(piece, piece, rs_sem.at[index], rr_sem.at[index], target)

    def r_arrival(side, s, chunk):
        piece = r_piece(wrap(z - sg * s) if side == 0 else wrap(z + sg * s), chunk)
        index = ((side * A) + s - 1) * chunks + chunk
        copy(piece, piece, rs_sem.at[index], rr_sem.at[index], ahead).wait_recv()

    started, arrived = set(), set()

    def r_step(n):
        s, chunk = n // chunks + 1, n % chunks
        for side, last in ((0, A), (1, B)):
            if s <= last:
                r_arrival(side, s, chunk)
                arrived.add((side, s, chunk))
                if s < last:
                    r_copy(side, s + 1, chunk).start()
                    started.add((side, s + 1, chunk))


    def finish(level):
        g_copy.wait_send()
        spread_wait(l_in, l_all, ls_sem, lr_sem)
        share_sent(l_all, lfs_sem, lfr_sem)
        for key in sorted(started - arrived):
            r_arrival(*key)
        for key in sorted(started):
            r_copy(*key).wait_send()
        for side, last in ((0, A), (1, B)):
            for s in range(1, last + 1):
                if level >= 4:
                    t_copy(side, s)[1].wait_send()
                if level >= 8:
                    for i in range(2):
                        d_copy(side, s, i).wait_send()
        if level >= 5:
            spread_wait(t_own, t_all, ts_sem, tr_sem)
            share_sent(t_all, tfs_sem, tfr_sem)
        if 3 <= level < 6:
            for made in moment_copies:
                made.wait()
        if level < 3:
            loads[3].wait()
            loads[4].wait()
        if level >= 6:
            for i in range(2):
                x_copy(i).wait_send()
        if level >= 9:
            b_copy.wait_send()
        if level >= 7:
            for i in range(2):
                for j in range(Y):
                    sib_copy(j, i).wait_send()
                for t in range(2 * Y):
                    made, here = u_copy(t, i)

                    @pl.when(jnp.logical_not(here))
                    def _():
                        made.wait_send()

    g_copy = copy(g_own, g_all.at[rows_me, :], g_sem.at[0], g_sem.at[1], partner)
    if not R_FIRST:
        g_copy.start()
        spread(l_in, l_all, ls_sem, lr_sem)
    loads[2].wait()
    for chunk in range(chunks):
        for side, last in ((0, A), (1, B)):
            if last:
                r_copy(side, 1, chunk).start()
                started.add((side, 1, chunk))
    if R_FIRST:
        g_copy.start()
        spread(l_in, l_all, ls_sem, lr_sem)
    steps = A * chunks
    done = 0

    def r_steps(count):
        nonlocal done
        for _ in range(count):
            if done < steps:
                r_step(done)
                done += 1

    share(l_in, l_all, ls_sem, lr_sem, lfs_sem, lfr_sem)
    r_steps(R_START)
    g_copy.wait_recv()
    share_wait(l_all, lfs_sem, lfr_sem)

    loads[3].wait()
    loads[4].wait()
    moment_copies = [
        copy(m_in.at[rows_me, :], m_in.at[rows_me, :], mv_sem.at[0], mv_sem.at[1], partner),
        copy(v_in.at[rows_me, :], v_in.at[rows_me, :], mv_sem.at[2], mv_sem.at[3], partner),
    ]
    for made in moment_copies:
        made.start()

    per = Z // K

    def part_body(i, _):
        k = lax.rem(z // per + K // 2 + i, K)
        value = lax.dot_general(
            l_all[k], g_all[...], (((0,), (0,)), ((), ())), preferred_element_type=F32
        ).astype(BF16)
        for j in range(per):
            part[k * per + j] = value[j * mr:(j + 1) * mr, :]
        return 0

    lax.fori_loop(0, K, part_body, 0)

    def t_copy(side, s):
        if side == 0:
            d = wrap(z + sg * (A + 1 - s))
            return d, copy(part.at[d], from_a.at[s - 1], tas_sem.at[s - 1], tar_sem.at[s - 1], ahead)
        d = wrap(z - sg * (B + 1 - s))
        return d, copy(part.at[d], from_b.at[s - 1], tbs_sem.at[s - 1], tbr_sem.at[s - 1], behind)

    for s in range(1, A + 1):
        for side, last, came in ((0, A, from_a), (1, B, from_b)):
            if s <= last:
                d, send = t_copy(side, s)
                if s > 1:
                    t_copy(side, s - 1)[1].wait_recv()
                    part[d] = (part[d].astype(F32) + came[s - 2].astype(F32)).astype(BF16)
                send.start()
        r_steps(R_FILL[(s - 1) % len(R_FILL)])
    total = part[z].astype(F32)
    if B:
        t_copy(1, B)[1].wait_recv()
        total = total + from_b[B - 1].astype(F32)
    t_copy(0, A)[1].wait_recv()
    total = total + from_a[A - 1].astype(F32)
    t_own[...] = total.astype(BF16)

    @pl.when(mine)
    def _():
        t_all[slot_me, rows_me, :] = t_own[...]

    spread(t_own, t_all, ts_sem, tr_sem)
    r_steps((steps - done) // 2)
    share(t_own, t_all, ts_sem, tr_sem, tfs_sem, tfr_sem)
    r_steps(steps)
    share_wait(t_all, tfs_sem, tfr_sem)

    nc = r_ref.shape[1]
    split = (nc // 2 + 127) // 128 * 128
    cuts = (slice(0, split), slice(split, nc))

    def x_copy(i):
        return copy(b_out.at[:, cuts[i]], b_in.at[:, cuts[i]], x_sem.at[2 * i], x_sem.at[2 * i + 1], partner)

    for i, cut in enumerate(cuts):
        acc = jnp.zeros((2 * mr, cut.stop - cut.start), F32)
        for k in range(K):
            right = r_all[pl.ds(k * per, per), :, cut].reshape(per * r_ref.shape[0], cut.stop - cut.start)
            acc = acc + jnp.dot(t_all[k], right, preferred_element_type=F32)
        x_out[:, cut] = acc
        b_out[:, cut] = acc.astype(BF16)
        x_copy(i).start()

    first_fix = 1.0 - beta_first**STEP
    second_fix = 1.0 - beta_second**STEP
    for made in moment_copies:
        made.wait()
    for i, cut in enumerate(cuts):
        x_copy(i).wait_recv()
        rotated = x_out[:, cut] + b_in[:, cut].astype(F32)
        new_moment = beta_first * m_in[:, cut] + (1.0 - beta_first) * rotated
        new_second = beta_second * v_in[:, cut] + (1.0 - beta_second) * rotated * rotated
        direction = new_moment / first_fix / (jnp.sqrt(new_second / second_fix) + epsilon_add)
        d_own[:, cut] = direction.astype(BF16)
        m_in[:, cut] = new_moment
        v_in[:, cut] = new_second
    rr = r_ref.shape[0]

    def update_block(k, cut):
        right = r_all[pl.ds(k * per, per)].reshape(per * rr, nc)[cut]
        return lax.dot_general(d_own[...], right, (((1,), (1,)), ((), ())), preferred_element_type=F32)

    def sib_copy(j, i):
        n = j * 2 + i
        return copy(sib_out.at[j, :, cuts[i]], sib_in.at[j, :, cuts[i]], ss_sem.at[n], sr_sem.at[n], sibling)

    for i, cut in enumerate(cuts):
        for j in range(Y):
            sib_out[j, :, cut] = update_block(j * C + 1 - core, cut).astype(BF16)
            sib_copy(j, i).start()

    def u_copy(t, i):
        txh, ty = t // Y, t % Y
        here = jnp.logical_and(mine, jnp.logical_and(txh == xh, ty == y))
        made = copy(
            u_out.at[ty, pl.ds(txh * mr, mr), cuts[i]], u_in.at[xl * Y + y, :, cuts[i]],
            us_sem.at[t * 2 + i], ur_sem.at[(xl * Y + y) * 2 + i], device(txh, z, xh, ty, core),
        )
        return made, here

    for i, cut in enumerate(cuts):
        for j in range(Y):
            value = update_block(j * C + core, cut)
            sib_copy(j, i).wait_recv()
            u_out[j, :, cut] = (value + sib_in[j, :, cut].astype(F32)).astype(BF16)
            for txh in range(2):
                made, here = u_copy(txh * Y + j, i)

                @pl.when(jnp.logical_not(here))
                def _():
                    made.start()

        @pl.when(mine)
        def _():
            u_in[xl * Y + y, :, cut] = u_out[y, rows_me, cut]

    nm_ref[...] = m_in[rows_me, :]
    nv_ref[...] = v_in[rows_me, :]

    def d_piece(owner, i):
        return d_all.at[owner // per, pl.ds(pl.multiple_of(lax.rem(owner, per) * mr, mr), mr), cuts[i]]

    def d_copy(side, s, i):
        owner, target = (wrap(z - sg * (s - 1)), ahead) if side == 0 else (wrap(z + sg * (s - 1)), behind)
        index = (side * A + s - 1) * 2 + i
        piece = d_piece(owner, i)
        return copy(piece, piece, d_sem_s.at[index], d_sem_r.at[index], target)

    def d_step(s, i):
        for side, last in ((0, A), (1, B)):
            if 1 <= s <= last:
                piece = d_piece(wrap(z - sg * s) if side == 0 else wrap(z + sg * s), i)
                index = (side * A + s - 1) * 2 + i
                copy(piece, piece, d_sem_s.at[index], d_sem_r.at[index], ahead).wait_recv()
            if s < last:
                d_copy(side, s + 1, i).start()

    def own_sum(i):
        cut = cuts[i]
        total = jnp.zeros((mr, cut.stop - cut.start), F32)
        for t in range(2 * Y):
            here = jnp.logical_and(mine, jnp.logical_and(t // Y == xl, t % Y == y))

            @pl.when(jnp.logical_not(here))
            def _():
                copy(
                    u_in.at[t, :, cut], u_in.at[t, :, cut], us_sem.at[0], ur_sem.at[t * 2 + i], sibling
                ).wait_recv()

            total = total + u_in[t, :, cut].astype(F32)
        d_all[z // per, pl.ds(pl.multiple_of(lax.rem(z, per) * mr, mr), mr), cut] = total.astype(BF16)

    own_sum(0)
    d_step(0, 0)
    for s in range(1, E_EARLY + 1):
        d_step(s, 0)
    own_sum(1)
    d_step(0, 1)
    for s in range(1, A + 1):
        if s + E_EARLY <= A:
            d_step(s + E_EARLY, 0)
        d_step(s, 1)
    rows_other = pl.ds(pl.multiple_of((1 - xh) * mr, mr), mr)
    acc = jnp.zeros((2 * mr, nc), F32)
    for k in range(K):
        acc = acc + jnp.dot(l_all[k], d_all[k], preferred_element_type=F32)
    x_out[...] = acc
    f_out[...] = x_out[rows_other, :].astype(BF16)
    b_copy = copy(f_out, f_in, b_sem.at[0], b_sem.at[1], partner)
    b_copy.start()
    b_copy.wait_recv()
    up_ref[...] = x_out[rows_me, :] + f_in[...].astype(F32)
    finish(9)


def per_device(Z, Y, gradient, moment, second, left_basis, right_basis):
    mr, nc = gradient.shape
    K = 2 * Y
    A, B = Z // 2, Z - 1 - Z // 2
    rr = right_basis.shape[0]
    lc = left_basis.shape[1]
    per = Z // K
    chunks = rr // mr
    V = pltpu.VMEM
    DMA = pltpu.SemaphoreType.DMA
    vmem = pl.BlockSpec(memory_space=pltpu.VMEM)
    out = jax.ShapeDtypeStruct((mr, nc), F32)
    return pl.pallas_call(
        functools.partial(optimizer_kernel, Z, Y),
        out_shape=(out, out, out),
        in_specs=[pl.BlockSpec(memory_space=pltpu.HBM)] * 5,
        out_specs=(vmem, vmem, vmem),
        scratch_shapes=[
            V((mr, nc), BF16),
            V((2 * mr, nc), BF16),
            V((K, 2 * mr, lc), BF16),
            V((Z, rr, nc), BF16),
            V((Z, mr, nc), BF16),
            V((A, mr, nc), BF16),
            V((max(B, 1), mr, nc), BF16),
            V((mr, nc), BF16),
            V((K, 2 * mr, nc), BF16),
            V((mr, nc), F32),
            V((2 * mr, nc), F32),
            V((2 * mr, nc), F32),
            V((mr, lc), BF16),
            V((2 * mr, nc), F32),
            V((mr, nc), BF16),
            V((mr, nc), BF16),
            V((2 * mr, nc), BF16),
            V((K, per * mr, nc), BF16),
            V((2 * mr, nc), BF16),
            V((2 * mr, nc), BF16),
            V((Y, 2 * mr, nc), BF16),
            V((Y, 2 * mr, nc), BF16),
            V((Y, 2 * mr, nc), BF16),
            V((2 * Y, mr, nc), BF16),
            DMA((5,)),
            DMA((3,)),
            DMA((2,)),
            DMA((2 * Y,)), DMA((2 * Y,)), DMA((2 * Y,)), DMA((2 * Y,)),
            DMA(((A + B) * chunks,)), DMA(((A + B) * chunks,)),
            DMA((A,)), DMA((A,)), DMA((max(B, 1),)), DMA((max(B, 1),)),
            DMA((2 * Y,)), DMA((2 * Y,)), DMA((2 * Y,)), DMA((2 * Y,)),
            DMA((4,)),
            DMA((2 * A + 2 * B,)), DMA((2 * A + 2 * B,)),
            DMA((2,)),
            DMA((2 * Y,)), DMA((2 * Y,)),
            DMA((4 * Y,)), DMA((4 * Y,)),
            DMA((4,)),
        ],
        compiler_params=pltpu.CompilerParams(
            collective_id=0, has_side_effects=True, vmem_limit_bytes=int(63.5 * 1024 * 1024)
        ),
    )(gradient, moment, second, left_basis, right_basis)


def solution(mesh):
    Z, Y = mesh.shape["row"] // 2, mesh.shape["col"] // 4
    return jax.shard_map(
        functools.partial(per_device, Z, Y),
        mesh=mesh,
        in_specs=(
            P("row", "col"),
            P("row", "col"),
            P("row", "col"),
            P("row", "col"),
            P("row", "col"),
        ),
        out_specs=(P("row", "col"), P("row", "col"), P("row", "col")),
        check_vma=False,
    )
```

time: 169 us -> 158 us (0.935)
  the two profiles are of different devices: /device:TPU:29 before, /device:TPU:8 now
where the time goes in v2:
time: 158 us
  Pallas kernels  154 us (97%)
  local copies, waits for them, and re-layouts  3.4 us (2%)
    pallas_call x1, Pallas kernels, per_device(): pl.pallas_call(functools.partial(optimizer_kernel, Z, Y), out_shape=(out,...  154 us
    unnamed x7, local copies, waits for them, and re-layouts  3.4 us

profile of v2, /device:TPU:8, one launch (start us, length us, event | category | flops | bytes accessed | tf_op | source)
XLA Modules:
  0.0 157.8 jit_solution(7104940943824951101)
XLA Ops:
  0.6 153.7 %shard_map.76 = (f32[112,448]{1,0:T(8,128)}, f32[112,448]{1,0:T(8,128)}, f32[112,448]{1,0:T(8,128)}) custom-call(f32[112,448]{1,0:T(8,128)} %g_ref.1, f32[112,448]{1,0:T(8,128)} %m_ref.1, f32[112,448]{1,0:T(8,128)} %v_ref.1, bf16[112,224]{1,0:T(8,128)(2,1)} %l_ref.1, bf16[224,448]{1,0:T(8,128)(2,1)} %r_ref.1), custom_call_target="tpu_custom_call" | custom-call | tf_op jit(solution)/shard_map/pallas_call | solution.py:442
  154.4 0.0 copy-start.1
  154.4 1.7 %copy.11 = f32[112,448]{1,0:T(8,128)} copy(f32[112,448]{1,0:T(8,128)} %get-tuple-element.6) | data formatting | bytes 401408
  156.1 0.0 copy-done.1
  156.1 0.0 copy-start
  156.1 0.7 copy.12
  156.7 0.3 copy-done
  157.1 0.7 copy.13
Async XLA Ops:
  154.4 1.7 %copy-start.1 = (f32[112,448]{1,0:T(8,128)S(1)}, f32[112,448]{1,0:T(8,128)}, u32[]{:S(2)}) copy-start(f32[112,448]{1,0:T(8,128)} %get-tuple-element.7) | copy-start | bytes 602116
  156.1 1.0 copy-start

commit v3 on v2

--- a/solution.py
+++ b/solution.py
@@ -22,12 +22,43 @@
 BF16 = jnp.bfloat16
 
 
+def tail_rows(rows):
+    return (rows // 2 + 15) // 16 * 16
+
+
+def packed_rows(rows, columns):
+    return columns // 128 * rows + (tail_rows(rows) if columns % 128 else 0)
+
+
+def pack(dst, value, columns, first=0):
+    rows = value.shape[0]
+    for start in range(first, first + value.shape[1], 128):
+        top, part = start // 128 * rows, value[:, start - first:min(start + 128, columns) - first]
+        if start + 128 <= columns:
+            dst[top:top + rows, :] = part
+        else:
+            h = tail_rows(rows)
+            dst[top:top + h, 0:64] = part[0:h]
+            dst[top:top + rows - h, 64:128] = part[h:rows]
+
+
+def unpack(dst, src, rows, columns):
+    for start in range(0, columns, 128):
+        top = start // 128 * rows
+        if start + 128 <= columns:
+            dst[:, start:start + 128] = src[top:top + rows, :]
+        else:
+            h = tail_rows(rows)
+            dst[0:h, start:columns] = src[top:top + h, 0:64]
+            dst[h:rows, start:columns] = src[top:top + rows - h, 64:128]
+
+
 def optimizer_kernel(
     Z, Y,
     g_ref, m_ref, v_ref, l_ref, r_ref,
     nm_ref, nv_ref, up_ref,
-    g_own, g_all, l_all, r_all, part, from_a, from_b, t_own, t_all,
-    g_in, m_in, v_in, l_in, x_out, f_out, f_in, d_own, d_all, b_out, b_in, sib_out, sib_in, u_out, u_in,
+    g_own, g_all, l_all, r_all, r_pk, part, from_a, from_b, t_own, t_pk, t_all,
+    g_in, m_in, v_in, l_in, x_out, f_out, f_in, d_own, d_pk, d_all, b_out, b_in, sib_out, sib_in, u_out, u_in,
     in_sem, out_sem, g_sem, ls_sem, lr_sem, lfs_sem, lfr_sem, rs_sem, rr_sem,
     tas_sem, tar_sem, tbs_sem, tbr_sem, ts_sem, tr_sem, tfs_sem, tfr_sem,
     x_sem, d_sem_s, d_sem_r, b_sem, ss_sem, sr_sem, us_sem, ur_sem, mv_sem,
@@ -36,6 +67,8 @@
     K = Y * C
     A, B = Z // 2, Z - 1 - Z // 2
     mr = g_ref.shape[0]
+    rr, nc = r_ref.shape
+    pt = packed_rows(mr, nc)
     row, col = lax.axis_index("row"), lax.axis_index("col")
     xh, z = row // Z, lax.rem(row, Z)
     core = lax.rem(col, C)
@@ -104,13 +137,17 @@
         here = jnp.logical_and(mine, jnp.logical_and(sxh == xh, sy == y))
         return sxh, sy, jnp.logical_not(here)
 
+    def half(dst, side):
+        rows = dst.shape[1] // 2
+        return pl.ds(pl.multiple_of(side * rows, 16), rows)
+
     def spread(src, dst, send, recv):
         for t in range(2 * Y):
             target, remote = to_chips(t)
 
             @pl.when(remote)
             def _():
-                copy(src, dst.at[slot_me, rows_me, :], send.at[t], recv.at[xh * Y + y], target).start()
+                copy(src, dst.at[slot_me, half(dst, xh), :], send.at[t], recv.at[xh * Y + y], target).start()
 
     def spread_wait(src, dst, send, recv):
         for t in range(2 * Y):
@@ -118,17 +155,17 @@
 
             @pl.when(remote)
             def _():
-                copy(src, dst.at[slot_me, rows_me, :], send.at[t], recv.at[0], target).wait_send()
+                copy(src, dst.at[slot_me, half(dst, xh), :], send.at[t], recv.at[0], target).wait_send()
 
     def share_copy(dst, t, send, recv, c):
         sxh, sy = t // Y, t % Y
-        place = dst.at[sy * C + c, pl.ds(sxh * mr, mr), :]
+        place = dst.at[sy * C + c, half(dst, sxh), :]
         return copy(place, place, send.at[t], recv.at[t], sibling)
 
     def share(src, dst, send, recv, fsend, frecv):
         for t in range(2 * Y):
             sxh, sy, remote = from_chips(t)
-            place = dst.at[sy * C + core, pl.ds(sxh * mr, mr), :]
+            place = dst.at[sy * C + core, half(dst, sxh), :]
 
             @pl.when(remote)
             def _():
@@ -144,10 +181,12 @@
         for t in range(2 * Y):
             share_copy(dst, t, fsend, frecv, core).wait_send()
 
+    r_split = (packed_rows(rr, nc) // 2 + 15) // 16 * 16
+    r_cuts = ((0, r_split), (r_split, packed_rows(rr, nc) - r_split))
+    chunks = 2
+
     def r_piece(owner, chunk):
-        return r_all.at[owner, pl.ds(chunk * mr, mr), :]
-
-    chunks = r_ref.shape[0] // mr
+        return r_pk.at[owner, pl.ds(*r_cuts[chunk]), :]
 
     def r_copy(side, s, chunk):
         if side == 0:
@@ -173,6 +212,9 @@
                 if s < last:
                     r_copy(side, s + 1, chunk).start()
                     started.add((side, s + 1, chunk))
+                if chunk == chunks - 1:
+                    owner = wrap(z - sg * s) if side == 0 else wrap(z + sg * s)
+                    unpack(r_all.at[owner], r_pk.at[owner], rr, nc)
 
 
     def finish(level):
@@ -191,8 +233,8 @@
                     for i in range(2):
                         d_copy(side, s, i).wait_send()
         if level >= 5:
-            spread_wait(t_own, t_all, ts_sem, tr_sem)
-            share_sent(t_all, tfs_sem, tfr_sem)
+            spread_wait(t_own, t_pk, ts_sem, tr_sem)
+            share_sent(t_pk, tfs_sem, tfr_sem)
         if 3 <= level < 6:
             for made in moment_copies:
                 made.wait()
@@ -220,6 +262,7 @@
         g_copy.start()
         spread(l_in, l_all, ls_sem, lr_sem)
     loads[2].wait()
+    pack(r_pk.at[z], r_all[z], nc)
     for chunk in range(chunks):
         for side, last in ((0, A), (1, B)):
             if last:
@@ -260,7 +303,7 @@
             l_all[k], g_all[...], (((0,), (0,)), ((), ())), preferred_element_type=F32
         ).astype(BF16)
         for j in range(per):
-            part[k * per + j] = value[j * mr:(j + 1) * mr, :]
+            pack(part.at[k * per + j], value[j * mr:(j + 1) * mr, :], nc)
         return 0
 
     lax.fori_loop(0, K, part_body, 0)
@@ -291,15 +334,17 @@
 
     @pl.when(mine)
     def _():
-        t_all[slot_me, rows_me, :] = t_own[...]
-
-    spread(t_own, t_all, ts_sem, tr_sem)
+        t_pk[slot_me, half(t_pk, xh), :] = t_own[...]
+
+    spread(t_own, t_pk, ts_sem, tr_sem)
     r_steps((steps - done) // 2)
-    share(t_own, t_all, ts_sem, tr_sem, tfs_sem, tfr_sem)
+    share(t_own, t_pk, ts_sem, tr_sem, tfs_sem, tfr_sem)
+    share_wait(t_pk, tfs_sem, tfr_sem)
+    for k in range(K):
+        for side in range(2):
+            unpack(t_all.at[k, side * mr:(side + 1) * mr, :], t_pk.at[k, side * pt:(side + 1) * pt, :], mr, nc)
     r_steps(steps)
-    share_wait(t_all, tfs_sem, tfr_sem)
-
-    nc = r_ref.shape[1]
+
     split = (nc // 2 + 127) // 128 * 128
     cuts = (slice(0, split), slice(split, nc))
 
@@ -328,7 +373,8 @@
         d_own[:, cut] = direction.astype(BF16)
         m_in[:, cut] = new_moment
         v_in[:, cut] = new_second
-    rr = r_ref.shape[0]
+
+    packs = (slice(0, split // 128 * mr), slice(split // 128 * mr, pt))
 
     def update_block(k, cut):
         right = r_all[pl.ds(k * per, per)].reshape(per * rr, nc)[cut]
@@ -347,7 +393,7 @@
         txh, ty = t // Y, t % Y
         here = jnp.logical_and(mine, jnp.logical_and(txh == xh, ty == y))
         made = copy(
-            u_out.at[ty, pl.ds(txh * mr, mr), cuts[i]], u_in.at[xl * Y + y, :, cuts[i]],
+            u_out.at[ty, txh, packs[i], :], u_in.at[xl * Y + y, packs[i], :],
             us_sem.at[t * 2 + i], ur_sem.at[(xl * Y + y) * 2 + i], device(txh, z, xh, ty, core),
         )
         return made, here
@@ -356,7 +402,9 @@
         for j in range(Y):
             value = update_block(j * C + core, cut)
             sib_copy(j, i).wait_recv()
-            u_out[j, :, cut] = (value + sib_in[j, :, cut].astype(F32)).astype(BF16)
+            value = (value + sib_in[j, :, cut].astype(F32)).astype(BF16)
+            for txh in range(2):
+                pack(u_out.at[j, txh], value[txh * mr:(txh + 1) * mr], nc, cut.start)
             for txh in range(2):
                 made, here = u_copy(txh * Y + j, i)
 
@@ -366,13 +414,13 @@
 
         @pl.when(mine)
         def _():
-            u_in[xl * Y + y, :, cut] = u_out[y, rows_me, cut]
+            u_in[xl * Y + y, packs[i], :] = u_out[y, xh, packs[i], :]
 
     nm_ref[...] = m_in[rows_me, :]
     nv_ref[...] = v_in[rows_me, :]
 
     def d_piece(owner, i):
-        return d_all.at[owner // per, pl.ds(pl.multiple_of(lax.rem(owner, per) * mr, mr), mr), cuts[i]]
+        return d_pk.at[owner, packs[i], :]
 
     def d_copy(side, s, i):
         owner, target = (wrap(z - sg * (s - 1)), ahead) if side == 0 else (wrap(z + sg * (s - 1)), behind)
@@ -388,21 +436,26 @@
                 copy(piece, piece, d_sem_s.at[index], d_sem_r.at[index], ahead).wait_recv()
             if s < last:
                 d_copy(side, s + 1, i).start()
+            if i == 1 and 1 <= s <= last:
+                owner = wrap(z - sg * s) if side == 0 else wrap(z + sg * s)
+                unpack(d_all.at[owner], d_pk.at[owner], mr, nc)
 
     def own_sum(i):
-        cut = cuts[i]
-        total = jnp.zeros((mr, cut.stop - cut.start), F32)
+        rows = packs[i]
+        total = jnp.zeros((rows.stop - rows.start, 128), F32)
         for t in range(2 * Y):
             here = jnp.logical_and(mine, jnp.logical_and(t // Y == xl, t % Y == y))
 
             @pl.when(jnp.logical_not(here))
             def _():
                 copy(
-                    u_in.at[t, :, cut], u_in.at[t, :, cut], us_sem.at[0], ur_sem.at[t * 2 + i], sibling
+                    u_in.at[t, rows, :], u_in.at[t, rows, :], us_sem.at[0], ur_sem.at[t * 2 + i], sibling
                 ).wait_recv()
 
-            total = total + u_in[t, :, cut].astype(F32)
-        d_all[z // per, pl.ds(pl.multiple_of(lax.rem(z, per) * mr, mr), mr), cut] = total.astype(BF16)
+            total = total + u_in[t, rows, :].astype(F32)
+        d_pk[z, rows, :] = total.astype(BF16)
+        if i == 1:
+            unpack(d_all.at[z], d_pk.at[z], mr, nc)
 
     own_sum(0)
     d_step(0, 0)
@@ -417,7 +470,7 @@
     rows_other = pl.ds(pl.multiple_of((1 - xh) * mr, mr), mr)
     acc = jnp.zeros((2 * mr, nc), F32)
     for k in range(K):
-        acc = acc + jnp.dot(l_all[k], d_all[k], preferred_element_type=F32)
+        acc = acc + jnp.dot(l_all[k], d_all[pl.ds(k * per, per)].reshape(per * mr, nc), preferred_element_type=F32)
     x_out[...] = acc
     f_out[...] = x_out[rows_other, :].astype(BF16)
     b_copy = copy(f_out, f_in, b_sem.at[0], b_sem.at[1], partner)
@@ -434,7 +487,8 @@
     rr = right_basis.shape[0]
     lc = left_basis.shape[1]
     per = Z // K
-    chunks = rr // mr
+    chunks = 2
+    pt = packed_rows(mr, nc)
     V = pltpu.VMEM
     DMA = pltpu.SemaphoreType.DMA
     vmem = pl.BlockSpec(memory_space=pltpu.VMEM)
@@ -449,10 +503,12 @@
             V((2 * mr, nc), BF16),
             V((K, 2 * mr, lc), BF16),
             V((Z, rr, nc), BF16),
-            V((Z, mr, nc), BF16),
-            V((A, mr, nc), BF16),
-            V((max(B, 1), mr, nc), BF16),
-            V((mr, nc), BF16),
+            V((Z, packed_rows(rr, nc), 128), BF16),
+            V((Z, pt, 128), BF16),
+            V((A, pt, 128), BF16),
+            V((max(B, 1), pt, 128), BF16),
+            V((pt, 128), BF16),
+            V((K, 2 * pt, 128), BF16),
             V((K, 2 * mr, nc), BF16),
             V((mr, nc), F32),
             V((2 * mr, nc), F32),
@@ -462,13 +518,14 @@
             V((mr, nc), BF16),
             V((mr, nc), BF16),
             V((2 * mr, nc), BF16),
-            V((K, per * mr, nc), BF16),
+            V((Z, pt, 128), BF16),
+            V((Z, mr, nc), BF16),
             V((2 * mr, nc), BF16),
             V((2 * mr, nc), BF16),
             V((Y, 2 * mr, nc), BF16),
             V((Y, 2 * mr, nc), BF16),
-            V((Y, 2 * mr, nc), BF16),
-            V((2 * Y, mr, nc), BF16),
+            V((Y, 2, pt, 128), BF16),
+            V((2 * Y, pt, 128), BF16),
             DMA((5,)),
             DMA((3,)),
             DMA((2,)),

time: 158 us -> 153 us (0.968)
  Pallas kernels: 154 us -> 149 us
    pallas_call x1, Pallas kernels: 154 us -> 149 us  [per_device(): pl.pallas_call(functools.partial(optimizer_kernel, Z, Y), out_shape=(out,...]
where the time goes in v3:
time: 153 us
  Pallas kernels  149 us (97%)
  local copies, waits for them, and re-layouts  3.4 us (2%)
    pallas_call x1, Pallas kernels, per_device(): pl.pallas_call(functools.partial(optimizer_kernel, Z, Y), out_shape=(out,...  149 us
    unnamed x7, local copies, waits for them, and re-layouts  3.4 us

profile of v3, /device:TPU:8, one launch (start us, length us, event | category | flops | bytes accessed | tf_op | source)
XLA Modules:
  0.0 152.7 jit_solution(3024863879631444554)
XLA Ops:
  0.6 148.7 %shard_map.76 = (f32[112,448]{1,0:T(8,128)}, f32[112,448]{1,0:T(8,128)}, f32[112,448]{1,0:T(8,128)}) custom-call(f32[112,448]{1,0:T(8,128)} %g_ref.1, f32[112,448]{1,0:T(8,128)} %m_ref.1, f32[112,448]{1,0:T(8,128)} %v_ref.1, bf16[112,224]{1,0:T(8,128)(2,1)} %l_ref.1, bf16[224,448]{1,0:T(8,128)(2,1)} %r_ref.1), custom_call_target="tpu_custom_call" | custom-call | tf_op jit(solution)/shard_map/pallas_call | solution.py:496
  149.3 0.0 copy-start.1
  149.3 1.7 %copy.11 = f32[112,448]{1,0:T(8,128)} copy(f32[112,448]{1,0:T(8,128)} %get-tuple-element.6) | data formatting | bytes 401408
  151.0 0.0 copy-done.1
  151.0 0.0 copy-start
  151.0 0.7 copy.12
  151.7 0.3 copy-done
  152.0 0.7 copy.13
Async XLA Ops:
  149.3 1.7 %copy-start.1 = (f32[112,448]{1,0:T(8,128)S(1)}, f32[112,448]{1,0:T(8,128)}, u32[]{:S(2)}) copy-start(f32[112,448]{1,0:T(8,128)} %get-tuple-element.7) | copy-start | bytes 602116
  151.0 1.0 copy-start

commit v4 on v3

--- a/solution.py
+++ b/solution.py
@@ -8,7 +8,9 @@
 from jax.sharding import PartitionSpec as P
 
 STEP = 100
-R_START = 1
+R_START = 2
+R_AFTER = 1
+R_MID = 1
 E_EARLY = 0
 R_FIRST = True
 R_FILL = (1,)
@@ -228,7 +230,8 @@
         for side, last in ((0, A), (1, B)):
             for s in range(1, last + 1):
                 if level >= 4:
-                    t_copy(side, s)[1].wait_send()
+                    for i in range(2):
+                        t_copy(side, s, i)[1].wait_send()
                 if level >= 8:
                     for i in range(2):
                         d_copy(side, s, i).wait_send()
@@ -308,36 +311,45 @@
 
     lax.fori_loop(0, K, part_body, 0)
 
-    def t_copy(side, s):
+    t_half = (pt // 2 + 15) // 16 * 16
+    t_cuts = (slice(0, t_half), slice(t_half, pt))
+
+    def t_copy(side, s, i):
+        rows, n = t_cuts[i], (s - 1) * 2 + i
         if side == 0:
             d = wrap(z + sg * (A + 1 - s))
-            return d, copy(part.at[d], from_a.at[s - 1], tas_sem.at[s - 1], tar_sem.at[s - 1], ahead)
+            return d, copy(part.at[d, rows, :], from_a.at[s - 1, rows, :], tas_sem.at[n], tar_sem.at[n], ahead)
         d = wrap(z - sg * (B + 1 - s))
-        return d, copy(part.at[d], from_b.at[s - 1], tbs_sem.at[s - 1], tbr_sem.at[s - 1], behind)
+        return d, copy(part.at[d, rows, :], from_b.at[s - 1, rows, :], tbs_sem.at[n], tbr_sem.at[n], behind)
 
     for s in range(1, A + 1):
-        for side, last, came in ((0, A, from_a), (1, B, from_b)):
-            if s <= last:
-                d, send = t_copy(side, s)
-                if s > 1:
-                    t_copy(side, s - 1)[1].wait_recv()
-                    part[d] = (part[d].astype(F32) + came[s - 2].astype(F32)).astype(BF16)
-                send.start()
-        r_steps(R_FILL[(s - 1) % len(R_FILL)])
-    total = part[z].astype(F32)
-    if B:
-        t_copy(1, B)[1].wait_recv()
-        total = total + from_b[B - 1].astype(F32)
-    t_copy(0, A)[1].wait_recv()
-    total = total + from_a[A - 1].astype(F32)
-    t_own[...] = total.astype(BF16)
+        for i, rows in enumerate(t_cuts):
+            for side, last, came in ((0, A, from_a), (1, B, from_b)):
+                if s <= last:
+                    d, send = t_copy(side, s, i)
+                    if s > 1:
+                        t_copy(side, s - 1, i)[1].wait_recv()
+                        part[d, rows, :] = (
+                            part[d, rows, :].astype(F32) + came[s - 2, rows, :].astype(F32)
+                        ).astype(BF16)
+                    send.start()
+            if i == R_AFTER:
+                r_steps(R_FILL[(s - 1) % len(R_FILL)])
+    for i, rows in enumerate(t_cuts):
+        total = part[z, rows, :].astype(F32)
+        if B:
+            t_copy(1, B, i)[1].wait_recv()
+            total = total + from_b[B - 1, rows, :].astype(F32)
+        t_copy(0, A, i)[1].wait_recv()
+        total = total + from_a[A - 1, rows, :].astype(F32)
+        t_own[rows, :] = total.astype(BF16)
 
     @pl.when(mine)
     def _():
         t_pk[slot_me, half(t_pk, xh), :] = t_own[...]
 
     spread(t_own, t_pk, ts_sem, tr_sem)
-    r_steps((steps - done) // 2)
+    r_steps((steps - done) // R_MID if R_MID else 0)
     share(t_own, t_pk, ts_sem, tr_sem, tfs_sem, tfr_sem)
     share_wait(t_pk, tfs_sem, tfr_sem)
     for k in range(K):
@@ -531,7 +543,7 @@
             DMA((2,)),
             DMA((2 * Y,)), DMA((2 * Y,)), DMA((2 * Y,)), DMA((2 * Y,)),
             DMA(((A + B) * chunks,)), DMA(((A + B) * chunks,)),
-            DMA((A,)), DMA((A,)), DMA((max(B, 1),)), DMA((max(B, 1),)),
+            DMA((2 * A,)), DMA((2 * A,)), DMA((2 * max(B, 1),)), DMA((2 * max(B, 1),)),
             DMA((2 * Y,)), DMA((2 * Y,)), DMA((2 * Y,)), DMA((2 * Y,)),
             DMA((4,)),
             DMA((2 * A + 2 * B,)), DMA((2 * A + 2 * B,)),

time: 153 us -> 150 us (0.980)
  Pallas kernels: 149 us -> 145 us
    pallas_call x1, Pallas kernels: 149 us -> 145 us  [per_device(): pl.pallas_call(functools.partial(optimizer_kernel, Z, Y), out_shape=(out,...]
where the time goes in v4:
time: 150 us; the launch traced here: 149 us
  Pallas kernels  145 us (97%)
  local copies, waits for them, and re-layouts  3.4 us (2%)
    pallas_call x1, Pallas kernels, per_device(): pl.pallas_call(functools.partial(optimizer_kernel, Z, Y), out_shape=(out,...  145 us
    unnamed x7, local copies, waits for them, and re-layouts  3.4 us

profile of v4, /device:TPU:8, one launch (start us, length us, event | category | flops | bytes accessed | tf_op | source)
XLA Modules:
  0.0 149.4 jit_solution(5555851615392424496)
XLA Ops:
  0.6 145.3 %shard_map.76 = (f32[112,448]{1,0:T(8,128)}, f32[112,448]{1,0:T(8,128)}, f32[112,448]{1,0:T(8,128)}) custom-call(f32[112,448]{1,0:T(8,128)} %g_ref.1, f32[112,448]{1,0:T(8,128)} %m_ref.1, f32[112,448]{1,0:T(8,128)} %v_ref.1, bf16[112,224]{1,0:T(8,128)(2,1)} %l_ref.1, bf16[224,448]{1,0:T(8,128)(2,1)} %r_ref.1), custom_call_target="tpu_custom_call" | custom-call | tf_op jit(solution)/shard_map/pallas_call | solution.py:508
  146.0 0.0 copy-start.1
  146.0 1.7 %copy.11 = f32[112,448]{1,0:T(8,128)} copy(f32[112,448]{1,0:T(8,128)} %get-tuple-element.6) | data formatting | bytes 401408
  147.7 0.0 copy-done.1
  147.7 0.0 copy-start
  147.7 0.7 copy.12
  148.4 0.3 copy-done
  148.7 0.7 copy.13
Async XLA Ops:
  146.0 1.7 %copy-start.1 = (f32[112,448]{1,0:T(8,128)S(1)}, f32[112,448]{1,0:T(8,128)}, u32[]{:S(2)}) copy-start(f32[112,448]{1,0:T(8,128)} %get-tuple-element.7) | copy-start | bytes 602116
  147.7 1.0 copy-start

commit v5 on v4

--- a/solution.py
+++ b/solution.py
@@ -9,8 +9,8 @@
 
 STEP = 100
 R_START = 2
-R_AFTER = 1
 R_MID = 1
+T_N = 1
 E_EARLY = 0
 R_FIRST = True
 R_FILL = (1,)
@@ -230,7 +230,7 @@
         for side, last in ((0, A), (1, B)):
             for s in range(1, last + 1):
                 if level >= 4:
-                    for i in range(2):
+                    for i in range(T_N):
                         t_copy(side, s, i)[1].wait_send()
                 if level >= 8:
                     for i in range(2):
@@ -311,11 +311,11 @@
 
     lax.fori_loop(0, K, part_body, 0)
 
-    t_half = (pt // 2 + 15) // 16 * 16
-    t_cuts = (slice(0, t_half), slice(t_half, pt))
+    marks = [min(pt, (pt * n // T_N + 15) // 16 * 16) for n in range(T_N + 1)]
+    t_cuts = tuple(slice(a, b) for a, b in zip(marks, marks[1:]))
 
     def t_copy(side, s, i):
-        rows, n = t_cuts[i], (s - 1) * 2 + i
+        rows, n = t_cuts[i], (s - 1) * T_N + i
         if side == 0:
             d = wrap(z + sg * (A + 1 - s))
             return d, copy(part.at[d, rows, :], from_a.at[s - 1, rows, :], tas_sem.at[n], tar_sem.at[n], ahead)
@@ -333,7 +333,7 @@
                             part[d, rows, :].astype(F32) + came[s - 2, rows, :].astype(F32)
                         ).astype(BF16)
                     send.start()
-            if i == R_AFTER:
+            if i == T_N - 1:
                 r_steps(R_FILL[(s - 1) % len(R_FILL)])
     for i, rows in enumerate(t_cuts):
         total = part[z, rows, :].astype(F32)
@@ -480,15 +480,21 @@
             d_step(s + E_EARLY, 0)
         d_step(s, 1)
     rows_other = pl.ds(pl.multiple_of((1 - xh) * mr, mr), mr)
-    acc = jnp.zeros((2 * mr, nc), F32)
-    for k in range(K):
-        acc = acc + jnp.dot(l_all[k], d_all[pl.ds(k * per, per)].reshape(per * mr, nc), preferred_element_type=F32)
-    x_out[...] = acc
-    f_out[...] = x_out[rows_other, :].astype(BF16)
+
+    def left_product(rows):
+        acc = jnp.zeros((mr, nc), F32)
+        for k in range(K):
+            acc = acc + jnp.dot(
+                l_all[k, rows, :], d_all[pl.ds(k * per, per)].reshape(per * mr, nc), preferred_element_type=F32
+            )
+        return acc
+
+    f_out[...] = left_product(rows_other).astype(BF16)
     b_copy = copy(f_out, f_in, b_sem.at[0], b_sem.at[1], partner)
     b_copy.start()
+    own = left_product(rows_me)
     b_copy.wait_recv()
-    up_ref[...] = x_out[rows_me, :] + f_in[...].astype(F32)
+    up_ref[...] = own + f_in[...].astype(F32)
     finish(9)
 
 
@@ -543,7 +549,7 @@
             DMA((2,)),
             DMA((2 * Y,)), DMA((2 * Y,)), DMA((2 * Y,)), DMA((2 * Y,)),
             DMA(((A + B) * chunks,)), DMA(((A + B) * chunks,)),
-            DMA((2 * A,)), DMA((2 * A,)), DMA((2 * max(B, 1),)), DMA((2 * max(B, 1),)),
+            DMA((T_N * A,)), DMA((T_N * A,)), DMA((T_N * max(B, 1),)), DMA((T_N * max(B, 1),)),
             DMA((2 * Y,)), DMA((2 * Y,)), DMA((2 * Y,)), DMA((2 * Y,)),
             DMA((4,)),
             DMA((2 * A + 2 * B,)), DMA((2 * A + 2 * B,)),

time: 150 us -> 148 us (0.987)
  the two profiles are of different devices: /device:TPU:8 before, /device:TPU:22 now
where the time goes in v5:
time: 148 us
  Pallas kernels  144 us (97%)
  local copies, waits for them, and re-layouts  3.4 us (2%)
    pallas_call x1, Pallas kernels, per_device(): pl.pallas_call(functools.partial(optimizer_kernel, Z, Y), out_shape=(out,...  144 us
    unnamed x7, local copies, waits for them, and re-layouts  3.4 us

profile of v5, /device:TPU:22, one launch (start us, length us, event | category | flops | bytes accessed | tf_op | source)
XLA Modules:
  0.0 147.8 jit_solution(69889492140725100)
XLA Ops:
  0.6 143.8 %shard_map.76 = (f32[112,448]{1,0:T(8,128)}, f32[112,448]{1,0:T(8,128)}, f32[112,448]{1,0:T(8,128)}) custom-call(f32[112,448]{1,0:T(8,128)} %g_ref.1, f32[112,448]{1,0:T(8,128)} %m_ref.1, f32[112,448]{1,0:T(8,128)} %v_ref.1, bf16[112,224]{1,0:T(8,128)(2,1)} %l_ref.1, bf16[224,448]{1,0:T(8,128)(2,1)} %r_ref.1), custom_call_target="tpu_custom_call" | custom-call | tf_op jit(solution)/shard_map/pallas_call | solution.py:514
  144.4 0.0 copy-start.1
  144.4 1.7 %copy.11 = f32[112,448]{1,0:T(8,128)} copy(f32[112,448]{1,0:T(8,128)} %get-tuple-element.6) | data formatting | bytes 401408
  146.1 0.0 copy-done.1
  146.1 0.0 copy-start
  146.1 0.7 copy.12
  146.8 0.3 copy-done
  147.1 0.7 copy.13
Async XLA Ops:
  144.4 1.7 %copy-start.1 = (f32[112,448]{1,0:T(8,128)S(1)}, f32[112,448]{1,0:T(8,128)}, u32[]{:S(2)}) copy-start(f32[112,448]{1,0:T(8,128)} %get-tuple-element.7) | copy-start | bytes 602116
  146.1 1.0 copy-start

commit v6 on v5

--- a/solution.py
+++ b/solution.py
@@ -9,7 +9,6 @@
 
 STEP = 100
 R_START = 2
-R_MID = 1
 T_N = 1
 E_EARLY = 0
 R_FIRST = True
@@ -349,7 +348,7 @@
         t_pk[slot_me, half(t_pk, xh), :] = t_own[...]
 
     spread(t_own, t_pk, ts_sem, tr_sem)
-    r_steps((steps - done) // R_MID if R_MID else 0)
+    r_steps(max(steps - done - chunks, 0))
     share(t_own, t_pk, ts_sem, tr_sem, tfs_sem, tfr_sem)
     share_wait(t_pk, tfs_sem, tfr_sem)
     for k in range(K):

time: 148 us -> 148 us (level)
  the two profiles are of different devices: /device:TPU:22 before, /device:TPU:14 now
where the time goes in v6:
time: 148 us
  Pallas kernels  144 us (97%)
  local copies, waits for them, and re-layouts  3.4 us (2%)
    pallas_call x1, Pallas kernels, per_device(): pl.pallas_call(functools.partial(optimizer_kernel, Z, Y), out_shape=(out,...  144 us
    unnamed x7, local copies, waits for them, and re-layouts  3.4 us

profile of v6, /device:TPU:14, one launch (start us, length us, event | category | flops | bytes accessed | tf_op | source)
XLA Modules:
  0.0 147.8 jit_solution(13519643482867100510)
XLA Ops:
  0.6 143.8 %shard_map.76 = (f32[112,448]{1,0:T(8,128)}, f32[112,448]{1,0:T(8,128)}, f32[112,448]{1,0:T(8,128)}) custom-call(f32[112,448]{1,0:T(8,128)} %g_ref.1, f32[112,448]{1,0:T(8,128)} %m_ref.1, f32[112,448]{1,0:T(8,128)} %v_ref.1, bf16[112,224]{1,0:T(8,128)(2,1)} %l_ref.1, bf16[224,448]{1,0:T(8,128)(2,1)} %r_ref.1), custom_call_target="tpu_custom_call" | custom-call | tf_op jit(solution)/shard_map/pallas_call | solution.py:513
  144.4 0.0 copy-start.1
  144.4 1.7 %copy.11 = f32[112,448]{1,0:T(8,128)} copy(f32[112,448]{1,0:T(8,128)} %get-tuple-element.6) | data formatting | bytes 401408
  146.1 0.0 copy-done.1
  146.1 0.0 copy-start
  146.1 0.7 copy.12
  146.8 0.3 copy-done
  147.1 0.7 copy.13
Async XLA Ops:
  144.4 1.7 %copy-start.1 = (f32[112,448]{1,0:T(8,128)S(1)}, f32[112,448]{1,0:T(8,128)}, u32[]{:S(2)}) copy-start(f32[112,448]{1,0:T(8,128)} %get-tuple-element.7) | copy-start | bytes 602116
  146.1 1.0 copy-start
